TPU v7x, 512 devices: a whole 4x4x16 slice. The times are simulated.
512 devices in a mesh: samp: 16 (over z), var: 32 (over x, y, core).
Axes of the slice: x: 4, y: 4, z: 16, core: 2. Of those that a mesh axis runs over, the one named last changes fastest.
Arguments:
- dosage: bfloat16 [3072, 32768], P('samp', 'var'), may hold values from -5 to 5
- coefficients: bfloat16 [32768, 256], P('var'), as said below
- targets: bfloat16 [3072, 256], P('samp'), may hold values from -5 to 5
- mask_words: int32 [3072, 16], P('samp'), may hold values from 0 to 65535
- penalty: float32 [256], replicated, may hold values from 0.1 to 1.5
- past_steps: bfloat16 [8, 32768, 256], P(None, ('var', 'samp')), as said below
- past_changes: bfloat16 [8, 32768, 256], P(None, ('var', 'samp')), as said below
Outputs:
- updated: float32 [32768, 256], P(('var', 'samp'))
Inputs may be any that keep to these rules, and one draw needn't show every extreme that they name: `past_changes`: each stored change y_i has a positive inner product with its own step s_i. `past_steps`: steps and changes come as pairs drawn together. The coefficients are drawn together with the stored pairs.
All inputs are finite; a program needn't handle non-finite values.
Results may differ from a plain program's by a relative error of at most 0.00066.
Values may be sent and summed in bfloat16 or wider, within the bound.
A program may use at most 64 MiB of HBM per device.

v0:
```python
import jax
import jax.numpy as jnp
from jax import lax
from jax.sharding import PartitionSpec as P

step_size = 0.5


def unpack_mask(mask_words):
    shifts = jnp.arange(16, dtype=jnp.int32)
    flags = jnp.bitwise_and(jnp.right_shift(mask_words[:, :, None], shifts[None, None, :]), 1)
    return flags.reshape(mask_words.shape[0], -1).astype(jnp.float32)


def recursive_apply(gradient, past_steps, past_changes):
    count = past_steps.shape[0]
    pair_local = jnp.einsum(
        "mvk,mvk->m", past_steps, past_changes, preferred_element_type=jnp.float32
    )
    last_change = past_changes[count - 1].astype(jnp.float32)
    last_local = jnp.sum(last_change * last_change)
    pair_dots, last_norm = lax.psum((pair_local, last_local), ("samp", "var"))
    scaling = pair_dots[count - 1] / last_norm
    running = gradient
    forward_weights = [None] * count
    for i in reversed(range(count)):
        step_wide = past_steps[i].astype(jnp.float32)
        product = lax.psum(jnp.sum(step_wide * running), ("samp", "var"))
        forward_weights[i] = product / pair_dots[i]
        running = running - forward_weights[i] * past_changes[i].astype(jnp.float32)
    running = scaling * running
    for i in range(count):
        change_wide = past_changes[i].astype(jnp.float32)
        product = lax.psum(jnp.sum(change_wide * running), ("samp", "var"))
        running = running + (forward_weights[i] - product / pair_dots[i]) * past_steps[i].astype(
            jnp.float32
        )
    return running


def per_device(dosage, coefficients, targets, mask_words, penalty, past_steps, past_changes):
    var_count = lax.axis_size("var")
    scale = (dosage.shape[1] * var_count) ** (-0.5)
    observed = unpack_mask(mask_words)
    margin = (
        lax.psum(jnp.dot(dosage, coefficients, preferred_element_type=jnp.float32), "var") * scale
    )
    residual = (observed * (margin - targets.astype(jnp.float32))).astype(jnp.bfloat16)
    owned_count = dosage.shape[1] // lax.axis_size("samp")
    gradient = (
        lax.psum_scatter(
            lax.dot_general(
                dosage, residual, (((0,), (0,)), ((), ())), preferred_element_type=jnp.float32
            ),
            "samp",
            scatter_dimension=0,
            tiled=True,
        )
        * scale
    )
    direction = recursive_apply(gradient, past_steps, past_changes)
    first_owned = lax.axis_index("samp") * owned_count
    owned_coefs = lax.dynamic_slice_in_dim(coefficients, first_owned, owned_count, 0).astype(
        jnp.float32
    )
    moved = owned_coefs - step_size * direction
    limit = step_size * penalty[None, :]
    return moved - jnp.clip(moved, -limit, limit)


def solution(mesh):
    in_specs = (
        P("samp", "var"),
        P("var", None),
        P("samp", None),
        P("samp", None),
        P(),
        P(None, ("var", "samp"), None),
        P(None, ("var", "samp"), None),
    )
    out_specs = P(("var", "samp"), None)
    return jax.shard_map(
        per_device, mesh=mesh, in_specs=in_specs, out_specs=out_specs, check_vma=False
    )
```

profile of v0, /device:TPU:1, one launch (start us, length us, event | category | flops | bytes accessed | tf_op | source)
XLA Modules:
  0.0 1859.9 jit_solution(4022741216258788676)
XLA Ops:
  6.5 1.0 copy-done
  7.6 1.9 fusion.52
  10.5 135.3 %all-reduce.4.cloned.1.call-done = f32[192,256]{1,0:T(8,128)} async-done(((f32[192,256]{1,0:T(8,128)}), f32[192,256]{1,0:T(8,128)}) %all-reduce.4.cloned.1.call-update) | async-done | bytes 196624 | tf_op jit(solution)/shard_map/psum | solution.py:46
  145.8 1.3 convolution_bitcast_fusion
  147.0 1.3 copy.72
  148.4 0.9 copy-done.3
  152.8 56.1 %reduce-scatter.4.cloned.1.call-done = f32[64,256]{1,0:T(8,128)} async-done(((f32[1024,256]{1,0:T(8,128)}), f32[64,256]{1,0:T(8,128)}) %reduce-scatter.4.cloned.1.call-update) | async-done | bytes 65552
  208.9 0.9 copy.73
  210.5 111.4 %all-reduce.1 = (f32[]{:T(128)}, f32[8]{0:T(128)S(1)}) all-reduce(f32[]{:T(128)} %fusion.30, f32[8]{0:T(128)S(1)} %fusion), channel_id=1, replica_groups=mesh['samp'=16,'var'=32] {'samp','var'}, use_global_device_ids=true, to_apply=%region_6.0 | all-reduce | flops 9 | bytes 72 | tf_op jit(solution)/shard_map/psum | solution.py:28
  324.6 99.9 %psum.137 = f32[]{:T(128)} all-reduce(f32[]{:T(128)} %fusion.28), channel_id=1, replica_groups=mesh['samp'=16,'var'=32] {'samp','var'}, use_global_device_ids=true, to_apply=%region_8.0 | all-reduce | flops 1 | bytes 8 | tf_op jit(solution)/shard_map/psum | solution.py:28
  426.3 100.5 %psum.138 = f32[]{:T(128)} all-reduce(f32[]{:T(128)} %get-tuple-element.6), channel_id=1, replica_groups=mesh['samp'=16,'var'=32] {'samp','var'}, use_global_device_ids=true, to_apply=%region_10.0 | all-reduce | flops 1 | bytes 8 | tf_op jit(solution)/shard_map/psum | solution.py:28
  528.9 99.2 %psum.139 = f32[]{:T(128)} all-reduce(f32[]{:T(128)} %get-tuple-element.21), channel_id=1, replica_groups=mesh['samp'=16,'var'=32] {'samp','var'}, use_global_device_ids=true, to_apply=%region_12.0 | all-reduce | flops 1 | bytes 8 | tf_op jit(solution)/shard_map/psum | solution.py:28
  630.0 100.2 %psum.140 = f32[]{:T(128)} all-reduce(f32[]{:T(128)} %fusion.16), channel_id=1, replica_groups=mesh['samp'=16,'var'=32] {'samp','var'}, use_global_device_ids=true, to_apply=%region_14.0 | all-reduce | flops 1 | bytes 8 | tf_op jit(solution)/shard_map/psum | solution.py:28
  732.1 99.3 %psum.141 = f32[]{:T(128)} all-reduce(f32[]{:T(128)} %get-tuple-element.19), channel_id=1, replica_groups=mesh['samp'=16,'var'=32] {'samp','var'}, use_global_device_ids=true, to_apply=%region_16.0 | all-reduce | flops 1 | bytes 8 | tf_op jit(solution)/shard_map/psum | solution.py:28
  833.5 100.2 %psum.142 = f32[]{:T(128)} all-reduce(f32[]{:T(128)} %fusion.8), channel_id=1, replica_groups=mesh['samp'=16,'var'=32] {'samp','var'}, use_global_device_ids=true, to_apply=%region_18.0 | all-reduce | flops 1 | bytes 8 | tf_op jit(solution)/shard_map/psum | solution.py:28
  935.5 99.5 %all-reduce = (f32[]{:T(128)}, f32[]{:T(128)}) all-reduce(f32[]{:T(128)} %get-tuple-element.17, f32[]{:T(128)} %get-tuple-element.5), channel_id=1, replica_groups=mesh['samp'=16,'var'=32] {'samp','var'}, use_global_device_ids=true, to_apply=%region_20.0 | all-reduce | flops 2 | bytes 16 | tf_op jit(solution)/shard_map/psum | solution.py:28
  1038.4 100.2 %psum.144 = f32[]{:T(128)} all-reduce(f32[]{:T(128)} %fusion.3), channel_id=1, replica_groups=mesh['samp'=16,'var'=32] {'samp','var'}, use_global_device_ids=true, to_apply=%region_22.0 | all-reduce | flops 1 | bytes 8 | tf_op jit(solution)/shard_map/psum | solution.py:34
  1140.7 99.4 %psum.145 = f32[]{:T(128)} all-reduce(f32[]{:T(128)} %get-tuple-element.15), channel_id=1, replica_groups=mesh['samp'=16,'var'=32] {'samp','var'}, use_global_device_ids=true, to_apply=%region_24.0 | all-reduce | flops 1 | bytes 8 | tf_op jit(solution)/shard_map/psum | solution.py:34
  1242.0 100.2 %psum.146 = f32[]{:T(128)} all-reduce(f32[]{:T(128)} %fusion.11), channel_id=1, replica_groups=mesh['samp'=16,'var'=32] {'samp','var'}, use_global_device_ids=true, to_apply=%region_26.0 | all-reduce | flops 1 | bytes 8 | tf_op jit(solution)/shard_map/psum | solution.py:34
  1344.1 99.6 %psum.147 = f32[]{:T(128)} all-reduce(f32[]{:T(128)} %fusion.15), channel_id=1, replica_groups=mesh['samp'=16,'var'=32] {'samp','var'}, use_global_device_ids=true, to_apply=%region_28.0 | all-reduce | flops 1 | bytes 8 | tf_op jit(solution)/shard_map/psum | solution.py:34
  1445.7 100.2 %psum.148 = f32[]{:T(128)} all-reduce(f32[]{:T(128)} %get-tuple-element.13), channel_id=1, replica_groups=mesh['samp'=16,'var'=32] {'samp','var'}, use_global_device_ids=true, to_apply=%region_30.0 | all-reduce | flops 1 | bytes 8 | tf_op jit(solution)/shard_map/psum | solution.py:34
  1547.8 99.4 %psum.149 = f32[]{:T(128)} all-reduce(f32[]{:T(128)} %fusion.23), channel_id=1, replica_groups=mesh['samp'=16,'var'=32] {'samp','var'}, use_global_device_ids=true, to_apply=%region_32.0 | all-reduce | flops 1 | bytes 8 | tf_op jit(solution)/shard_map/psum | solution.py:34
  1649.2 100.2 %psum.150 = f32[]{:T(128)} all-reduce(f32[]{:T(128)} %get-tuple-element.11), channel_id=1, replica_groups=mesh['samp'=16,'var'=32] {'samp','var'}, use_global_device_ids=true, to_apply=%region_34.0 | all-reduce | flops 1 | bytes 8 | tf_op jit(solution)/shard_map/psum | solution.py:34
  1751.4 99.4 %psum.151 = f32[]{:T(128)} all-reduce(f32[]{:T(128)} %fusion.36), channel_id=1, replica_groups=mesh['samp'=16,'var'=32] {'samp','var'}, use_global_device_ids=true, to_apply=%region_36.0 | all-reduce | flops 1 | bytes 8 | tf_op jit(solution)/shard_map/psum | solution.py:34
  (61 shorter events, 16.2 us)
Async XLA Ops:
  6.5 1.0 copy-start
  6.5 139.2 %all-reduce.4.cloned.1.call-start = ((), (), s32[]{:S(2)}) async-start(), calls=%async_computation.1 | async-start | bytes 393216 | tf_op jit(solution)/shard_map/psum | solution.py:46
  9.5 0.7 copy-start.5
  9.5 136.2 %copy-start.1 = (bf16[192,1024]{1,0:T(8,128)(2,1)S(1)}, bf16[192,1024]{1,0:T(8,128)(2,1)}, u32[]{:S(2)}) copy-start(bf16[192,1024]{1,0:T(8,128)(2,1)} %param.7) | copy-start | bytes 1179652
  9.6 199.3 %reduce-scatter.4.cloned.1.call-start = ((), (), s32[]{:S(2)}) async-start(), calls=%async_computation.2 | async-start | bytes 1114112
  10.3 135.5 %copy-start.4 = (bf16[192,256]{1,0:T(8,128)(2,1)S(1)}, bf16[192,256]{1,0:T(8,128)(2,1)}, u32[]{:S(2)}) copy-start(bf16[192,256]{1,0:T(8,128)(2,1)} %param.9) | copy-start | bytes 294916
  148.4 0.9 copy-start.3
  149.3 0.9 copy-start.2
  152.1 0.7 copy-start.6
Sparse Core Ops, SparseCore 0:
  10.6 135.1 all-reduce.3
  148.8 60.0 reduce-scatter.3
where the time goes:
time: 1860 us
  blocking collectives  1610 us (87%)
  waiting for transfers between devices  191 us (10%)
  between operations  36 us (2%)
    psum x8, blocking collectives, recursive_apply(): product = lax.psum(jnp.sum(step_wide * running), ('samp', 'var'))  810 us
    psum x8, blocking collectives, recursive_apply(): product = lax.psum(jnp.sum(change_wide * running), ('samp', 'var'))  799 us
    psum x1, waiting for transfers between devices, per_device(): lax.psum(jnp.dot(dosage, coefficients, preferred_element_type=jnp.float32...  135 us
    unnamed x3, waiting for transfers between devices  56.1 us
  transfers between devices with their start and end apart: 2, of which 2 were waited for; matrix products, arithmetic and copies ran while one was open for 0% of the time, Pallas kernels for 0%

commit v1 on v0

v1 whole, which is shorter than its diff:
```python
import functools

import jax
import jax.numpy as jnp
from jax import lax
from jax.experimental import pallas as pl
from jax.experimental.pallas import tpu as pltpu
from jax.sharding import PartitionSpec as P

MESH = pl.DeviceIdType.MESH
STEP = 0.5
ZN = 16
VN = 32
PAIRS = 8
UNITS = 12
OFFSET = [0] + [(s + 1) // 2 if s % 2 else -(s // 2) for s in range(1, ZN)]
GROUPS = [(0, 4), (4, 4), (8, 4), (12, 4)]
EARLY = 9


def wait_for(ref, sem):
    pltpu.make_async_copy(ref, ref, sem).wait()


def row_sum(block):
    return jnp.sum(block, axis=0)


def pair_index(i, j):
    return i * PAIRS - (i * (i - 1)) // 2 + (j - i)


def weight_rows(sums):
    lane = lax.broadcasted_iota(jnp.int32, (1, 128), 1)

    def entry(k):
        return jnp.broadcast_to(sums[:, k : k + 1], (1, 128))

    def unit(k):
        return jnp.where(lane == k, 1.0, 0.0)

    half = PAIRS * (PAIRS + 1) // 2
    upper = {(i, j): entry(pair_index(i, j)) for i in range(PAIRS) for j in range(i, PAIRS)}
    gram = {(i, j): entry(half + pair_index(i, j)) for i in range(PAIRS) for j in range(i, PAIRS)}
    scaling = upper[PAIRS - 1, PAIRS - 1] / gram[PAIRS - 1, PAIRS - 1]
    inner = [None] * PAIRS
    for i in reversed(range(PAIRS)):
        total = unit(i)
        for j in range(i + 1, PAIRS):
            total = total - upper[i, j] * inner[j]
        inner[i] = total / upper[i, i]
    outer = [None] * PAIRS
    for i in range(PAIRS):
        total = gram[min(i, 0), max(i, 0)] * inner[0]
        for j in range(1, PAIRS):
            total = total + gram[min(i, j), max(i, j)] * inner[j]
        total = upper[i, i] * inner[i] + scaling * total - scaling * unit(PAIRS + i)
        for j in range(i):
            total = total - upper[j, i] * outer[j]
        outer[i] = total / upper[i, i]
    return scaling, outer + [-scaling * row for row in inner]


def kernel(
    dosage_hbm,
    coef_hbm,
    target_hbm,
    mask_hbm,
    penalty_ref,
    steps_hbm,
    changes_hbm,
    out_ref,
    dosage,
    coef,
    target,
    mask,
    hist,
    part,
    tiles,
    x_all,
    x_turned,
    r_all,
    partial_in,
    hist_other,
    gram_acc,
    gram_own,
    gram_plane,
    gram_line,
    weights,
    gamma,
    g_acc,
    g_half,
    g_own,
    dots_own,
    dots_line,
    dots_mid,
    dots_plane,
    local_sem,
    part_send,
    part_recv,
    dose_send,
    dose_recv,
    swap_send,
    swap_recv,
    hist_send,
    hist_recv,
    gram_send,
    gram_recv,
    line_send,
    line_recv,
    res_send,
    res_recv,
    g_send,
    g_recv,
    dots_send,
    dots_recv,
):
    z = lax.axis_index("samp")
    v = lax.axis_index("var")
    core = lax.rem(v, 2)
    chip = lax.div(v, 2)
    other = 1 - core
    mate = v + 1 - 2 * core
    scale = (VN * dosage.shape[1]) ** -0.5

    def unit_of(c):
        x, y = lax.div(c, 4), lax.rem(c, 4)
        s = lax.rem(x + y, 4)
        return s < 3, 3 * x + jnp.minimum(s, 2)

    owner, mine = unit_of(chip)
    lanes = pl.ds(pl.multiple_of(core * 128, 128), 128)
    other_lanes = pl.ds(pl.multiple_of(other * 128, 128), 128)

    def at_z(s):
        return lax.rem(z - OFFSET[s] + ZN, ZN)

    def remote(src, dst, send, recv, zz, vv):
        return pltpu.make_async_remote_copy(
            src_ref=src, dst_ref=dst, send_sem=send, recv_sem=recv, device_id=(zz, vv), device_id_type=MESH
        )

    loads = [
        pltpu.make_async_copy(dosage_hbm, dosage, local_sem.at[0]),
        pltpu.make_async_copy(coef_hbm, coef, local_sem.at[1]),
        pltpu.make_async_copy(steps_hbm, hist.at[pl.ds(0, PAIRS)], local_sem.at[2]),
        pltpu.make_async_copy(changes_hbm, hist.at[pl.ds(PAIRS, PAIRS)], local_sem.at[3]),
        pltpu.make_async_copy(target_hbm, target, local_sem.at[4]),
        pltpu.make_async_copy(mask_hbm, mask, local_sem.at[5]),
    ]
    for load in loads:
        load.start()

    barrier = pltpu.get_barrier_semaphore()

    @pl.loop(1, VN)
    def _(r):
        pl.semaphore_signal(barrier, inc=1, device_id=(z, lax.rem(v + r, VN)), device_id_type=MESH)

    @pl.loop(1, ZN)
    def _(r):
        pl.semaphore_signal(barrier, inc=1, device_id=(lax.rem(z + r, ZN), v), device_id_type=MESH)

    loads[0].wait()
    loads[1].wait()
    product = jnp.dot(dosage[...], coef[...], preferred_element_type=jnp.float32)
    for u in range(UNITS):
        for h in range(2):
            part[u, h] = product[16 * u : 16 * u + 16, 128 * h : 128 * h + 128]
    for j in range(ZN // 2):
        top = dosage[0:96, 128 * j : 128 * j + 128]
        low = dosage[96:192, 128 * j : 128 * j + 128]
        tiles[2 * j] = jnp.concatenate([top[:, :64], low[:, :64]], axis=1)
        tiles[2 * j + 1] = jnp.concatenate([top[:, 64:], low[:, 64:]], axis=1)
    loads[2].wait()
    loads[3].wait()

    pl.semaphore_wait(barrier, VN - 1 + ZN - 1)

    @pl.loop(1, VN)
    def _(r):
        dest = lax.rem(v + r, VN)
        owns, u = unit_of(lax.div(dest, 2))

        @pl.when(owns)
        def _():
            remote(part.at[u, lax.rem(dest, 2)], partial_in.at[VN - 1 - r], part_send, part_recv, z, dest).start()

    def send_dosage(s):
        g = s // 4
        remote(tiles.at[at_z(s)], x_all.at[core, s], dose_send, dose_recv.at[g], at_z(s), v).start()

    for s in range(1, EARLY):
        send_dosage(s)
    hist_copy = remote(hist.at[:, :, other_lanes], hist_other, hist_send, hist_recv, z, mate)
    hist_copy.start()

    gram_acc[...] = jnp.zeros_like(gram_acc)
    half = PAIRS * (PAIRS + 1) // 2

    @pl.loop(0, 8)
    def _(t):
        rows = pl.ds(pl.multiple_of(lax.div(t, 2) * 16, 16), 16)
        cols = pl.ds(pl.multiple_of(lax.rem(t, 2) * 128, 128), 128)
        wide = [hist[i, rows, cols].astype(jnp.float32) for i in range(2 * PAIRS)]
        for i in range(PAIRS):
            for j in range(i, PAIRS):
                k = pair_index(i, j)
                one = wide[i] * wide[PAIRS + j]
                two = wide[PAIRS + i] * wide[PAIRS + j]
                gram_acc[k] += one[:8] + one[8:]
                gram_acc[half + k] += two[:8] + two[8:]

    folded = jnp.sum(gram_acc[...], axis=1)
    gram_own[0] = lax.dot_general(
        jnp.ones((8, 128), jnp.float32),
        folded,
        (((1,), (1,)), ((), ())),
        precision=lax.Precision.HIGHEST,
        preferred_element_type=jnp.float32,
    )[0:1]

    @pl.loop(1, VN)
    def _(r):
        remote(
            gram_own.at[0], gram_plane.at[VN - 1 - r], gram_send, gram_recv, z, lax.rem(v + r, VN)
        ).start()

    x_all[core, 0] = tiles[z]
    loads[4].wait()
    loads[5].wait()

    def spread(groups_from, count, g):
        @pl.loop(1, VN // 2)
        def _(r):
            block = r_all.at[pl.ds(groups_from, count), mine]
            remote(block, block, res_send.at[1], res_recv.at[4 + g], z, lax.rem(v + 2 * r, VN)).start()

    @pl.when(owner)
    def _():
        rows = pl.ds(pl.multiple_of(mine * 16, 16), 16)
        lane = lax.broadcasted_iota(jnp.int32, (16, 128), 1)
        word_at = jnp.right_shift(lane, 4) + 8 * core
        words = mask[rows, :]
        word = jnp.zeros((16, 128), jnp.int32)
        for w in range(16):
            word = jnp.where(word_at == w, jnp.broadcast_to(words[:, w : w + 1], (16, 128)), word)
        observed = jnp.bitwise_and(jnp.right_shift(word, jnp.bitwise_and(lane, 15)), 1).astype(jnp.float32)
        wanted = target[rows, lanes].astype(jnp.float32)
        wait_for(partial_in, part_recv)
        margin = (row_sum(partial_in[...]) + part[mine, core]) * scale
        r_all[0, mine] = (observed * (margin - wanted)).astype(jnp.bfloat16)
        for s in range(1, ZN):
            remote(r_all.at[0, mine], r_all.at[s, mine], res_send.at[0], res_recv.at[s // 4], at_z(s), v).start()
        spread(0, 1, 0)

    for s in range(EARLY, ZN):
        send_dosage(s)

    wait_for(gram_plane, gram_recv)
    gram_own[1] = row_sum(gram_plane[...]) + gram_own[0]
    for s in range(1, ZN):
        remote(gram_own.at[1], gram_line.at[s - 1], line_send.at[0], line_recv.at[0], at_z(s), v).start()

    def swap(g):
        first, count = GROUPS[g]
        skip = 1 if g == 0 else 0
        wait_for(x_all.at[core, pl.ds(first + skip, count - skip)], dose_recv.at[g])
        block = x_all.at[core, pl.ds(first, count)]
        remote(block, block, swap_send, swap_recv.at[g], z, mate).start()

    def pass_on(g):
        first, count = GROUPS[g]
        skip = 1 if g == 0 else 0

        @pl.when(owner)
        def _():
            wait_for(r_all.at[pl.ds(first + skip, count - skip), mine], res_recv.at[g])
            spread(first + skip, count - skip, g + 1)

    def turn(g):
        first, count = GROUPS[g]
        wait_for(x_all.at[other, pl.ds(first, count)], swap_recv.at[g])
        for c in range(2):
            x_turned[c, g] = x_all[c, first : first + count].reshape(count * 96, 128).T

    def residuals_here(first, count, g):
        @pl.when(owner)
        def _():
            wait_for(r_all.at[pl.ds(first, count), pl.ds(0, UNITS - 1)], res_recv.at[4 + g])

        @pl.when(jnp.logical_not(owner))
        def _():
            wait_for(r_all.at[pl.ds(first, count)], res_recv.at[4 + g])

    def multiply(g):
        first, count = GROUPS[g]
        if g == 0:
            residuals_here(0, 1, 0)
            residuals_here(1, count - 1, 1)
        else:
            residuals_here(first, count, g + 1)
        rows = jnp.concatenate(
            [
                r_all[first : first + count, 0:6].reshape(count * 96, 128),
                r_all[first : first + count, 6:12].reshape(count * 96, 128),
            ],
            axis=1,
        )
        for c in range(2):
            total = jnp.dot(x_turned[c, g], rows, preferred_element_type=jnp.float32)
            g_acc[c] = total if g == 0 else g_acc[c] + total

    swap(0)
    swap(1)
    pass_on(0)
    pass_on(1)
    turn(0)
    pass_on(2)
    turn(1)
    pass_on(3)
    multiply(0)
    multiply(1)
    swap(2)
    swap(3)
    turn(2)
    multiply(2)
    turn(3)
    multiply(3)

    for c in range(2):
        total = g_acc[c]
        g_half[c] = (total[:64, :128] + total[64:, 128:]) * scale
    g_copy = remote(g_half.at[other], g_own.at[core], g_send, g_recv, z, mate)
    g_copy.start()
    g_own[core] = g_half[core]

    near, far = g_half[core], g_half[other]
    hist_copy.wait_recv()
    sub = lax.broadcasted_iota(jnp.int32, (16, 128), 0)
    lane = lax.broadcasted_iota(jnp.int32, (16, 128), 1)
    folds = []
    for i in range(2 * PAIRS):
        both = hist[i, :, lanes].astype(jnp.float32) * near + hist_other[i].astype(jnp.float32) * far
        folds.append(jnp.sum(both, axis=0, keepdims=True))
    sums = jnp.sum(jnp.concatenate(folds, axis=0), axis=1, keepdims=True)
    dots_own[0] = jnp.sum(jnp.where(sub == lane, sums, 0.0), axis=0, keepdims=True)
    for s in range(1, ZN):
        remote(dots_own.at[0], dots_line.at[s - 1], line_send.at[1], line_recv.at[1], at_z(s), v).start()

    wait_for(gram_line, line_recv.at[0])
    scaling, rows = weight_rows(row_sum(gram_line[...]) + gram_own[1])
    gamma[...] = scaling
    for i in range(2 * PAIRS):
        weights[i : i + 1, :] = rows[i]
    g_copy.wait_recv()

    wait_for(dots_line, line_recv.at[1])
    dots_mid[0] = row_sum(dots_line[...]) + dots_own[0]

    @pl.loop(1, VN)
    def _(r):
        remote(
            dots_mid.at[0], dots_plane.at[VN - 1 - r], dots_send, dots_recv, z, lax.rem(v + r, VN)
        ).start()

    own_rows = pl.ds(pl.multiple_of(z * 64, 64), 64)
    start = coef[own_rows, :].astype(jnp.float32)
    gradient = jnp.concatenate([g_own[0], g_own[1]], axis=1)
    start = start - STEP * (gamma[0:1, 0:1] * gradient)
    limit = STEP * penalty_ref[...]

    wait_for(dots_plane, dots_recv)
    dots = row_sum(dots_plane[...]) + dots_mid[0]
    mix = jnp.sum(weights[...] * dots, axis=1, keepdims=True)
    along = mix[0:1] * hist[0].astype(jnp.float32)
    for i in range(1, 2 * PAIRS):
        along = along + mix[i : i + 1] * hist[i].astype(jnp.float32)
    moved = start - STEP * along
    out_ref[...] = moved - jnp.clip(moved, -limit, limit)

    @pl.when(owner)
    def _():
        wait_for(part.at[pl.ds(0, UNITS - 1)], part_send)
        wait_for(part.at[0, 0], part_send)
        wait_for(r_all.at[pl.ds(1, ZN - 1), 0], res_send.at[0])
        wait_for(r_all.at[pl.ds(0, ZN - 1), 0], res_send.at[1])
        for _ in range(ZN - 1):
            wait_for(r_all.at[pl.ds(1, ZN - 1), 0], res_send.at[1])

    @pl.when(jnp.logical_not(owner))
    def _():
        wait_for(part, part_send)

    wait_for(tiles.at[pl.ds(1, ZN - 1)], dose_send)
    wait_for(x_all.at[0], swap_send)
    hist_copy.wait_send()
    g_copy.wait_send()
    wait_for(gram_plane, gram_send)
    wait_for(gram_line, line_send.at[0])
    wait_for(dots_line, line_send.at[1])
    wait_for(dots_plane, dots_send)


def per_device(dosage, coefficients, targets, mask_words, penalty, past_steps, past_changes):
    samples, variants = dosage.shape
    traits = coefficients.shape[1]
    owned = variants // ZN
    f32, bf16 = jnp.float32, jnp.bfloat16
    vmem = pltpu.VMEM
    dma = pltpu.SemaphoreType.DMA
    anywhere = pl.BlockSpec(memory_space=pl.ANY)
    return pl.pallas_call(
        kernel,
        out_shape=jax.ShapeDtypeStruct((owned, traits), f32),
        in_specs=[anywhere] * 4 + [pl.BlockSpec(memory_space=vmem)] + [anywhere] * 2,
        out_specs=pl.BlockSpec(memory_space=vmem),
        scratch_shapes=[
            vmem((samples, variants), bf16),
            vmem((variants, traits), bf16),
            vmem((samples, traits), bf16),
            vmem(mask_words.shape, jnp.int32),
            vmem((2 * PAIRS, owned, traits), bf16),
            vmem((UNITS, 2, 16, 128), f32),
            vmem((ZN, 96, 128), bf16),
            vmem((2, ZN, 96, 128), bf16),
            vmem((2, 4, 128, 384), bf16),
            vmem((ZN, UNITS, 16, 128), bf16),
            vmem((VN - 1, 16, 128), f32),
            vmem((2 * PAIRS, owned, 128), bf16),
            vmem((128, 8, 128), f32),
            vmem((2, 1, 128), f32),
            vmem((VN - 1, 1, 128), f32),
            vmem((ZN - 1, 1, 128), f32),
            vmem((2 * PAIRS, 128), f32),
            vmem((1, 128), f32),
            vmem((2, 128, 256), f32),
            vmem((2, owned, 128), f32),
            vmem((2, owned, 128), f32),
            vmem((1, 1, 128), f32),
            vmem((ZN - 1, 1, 128), f32),
            vmem((1, 1, 128), f32),
            vmem((VN - 1, 1, 128), f32),
            dma((6,)),
            dma,
            dma,
            dma,
            dma((4,)),
            dma,
            dma((4,)),
            dma,
            dma,
            dma,
            dma,
            dma((2,)),
            dma((2,)),
            dma((2,)),
            dma((9,)),
            dma,
            dma,
            dma,
            dma,
        ],
        compiler_params=pltpu.CompilerParams(
            collective_id=0, has_side_effects=True, vmem_limit_bytes=48 * 1024 * 1024
        ),
    )(dosage, coefficients, targets, mask_words, penalty[None, :], past_steps, past_changes)


def solution(mesh):
    in_specs = (
        P("samp", "var"),
        P("var", None),
        P("samp", None),
        P("samp", None),
        P(),
        P(None, ("var", "samp"), None),
        P(None, ("var", "samp"), None),
    )
    out_specs = P(("var", "samp"), None)
    return jax.shard_map(
        per_device, mesh=mesh, in_specs=in_specs, out_specs=out_specs, check_vma=False
    )
```

time: 1860 us -> 64.4 us (0.03)
  blocking collectives: 1610 us -> 0 us
  waiting for transfers between devices: 191 us -> 0 us
  Pallas kernels: 0 us -> 58.6 us
  between operations: 36 us -> 0.02 us
    psum x16 -> x0, blocking collectives: 1610 us -> none  [the longest x8 810 us: recursive_apply(): product = lax.psum(jnp.sum(step_wide * running), ('samp', 'var'))]
    psum x1 -> x0, waiting for transfers between devices: 135 us -> none  [per_device(): lax.psum(jnp.dot(dosage, coefficients, preferred_element_type=jnp.float32...]
    pallas_call x0 -> x1, Pallas kernels: none -> 58.6 us  [per_device(): pl.pallas_call(kernel, out_shape=jax.ShapeDtypeStruct((owned, traits), f3...]
    unnamed x3 -> x0, waiting for transfers between devices: 56.1 us -> none
  transfers between devices with their start and end apart: 2 -> 0, of which waited for: 2 -> 0; matrix products, arithmetic and copies ran while one was open for 0% -> 0% of each run, Pallas kernels for 0% -> 0%
where the time goes in v1:
time: 64.4 us; the launch traced here: 64.1 us
  Pallas kernels  58.6 us (91%)
  local copies, waits for them, and re-layouts  5.48 us (9%)
    pallas_call x1, Pallas kernels, per_device(): pl.pallas_call(kernel, out_shape=jax.ShapeDtypeStruct((owned, traits), f3...  58.6 us
    unnamed x14, local copies, waits for them, and re-layouts  5.48 us

profile of v1, /device:TPU:1, one launch (start us, length us, event | category | flops | bytes accessed | tf_op | source)
XLA Modules:
  0.0 64.1 jit_solution(16314006827093358682)
XLA Ops:
  0.0 0.0 copy-start.4
  0.0 0.0 copy-start.5
  0.0 0.8 %copy.8.mask_hbm = s32[192,16]{1,0:T(8,128)S(1)} copy(s32[192,16]{0,1:T(8,128)} %param.10) | data formatting | bytes 24576 | tf_op args[3]
  0.9 0.1 copy-done.4
  0.9 0.0 copy-done.5
  0.9 0.0 copy-start
  0.9 1.0 %copy-done = bf16[1024,256]{1,0:T(8,128)(2,1)S(1)} copy-done((bf16[1024,256]{1,0:T(8,128)(2,1)S(1)}, bf16[1024,256]{1,0:T(8,128)(2,1)}, u32[]{:S(2)}) %copy-start) | copy-done | bytes 524312
  2.0 0.0 copy-start.1
  2.0 1.0 %copy-done.1 = bf16[192,1024]{1,0:T(8,128)(2,1)S(1)} copy-done((bf16[192,1024]{1,0:T(8,128)(2,1)S(1)}, bf16[192,1024]{1,0:T(8,128)(2,1)}, u32[]{:S(2)}) %copy-start.1) | copy-done | bytes 393240
  3.0 0.0 copy-start.2
  3.0 0.9 %copy-done.2 = bf16[8,64,256]{2,1,0:T(8,128)(2,1)S(1)} copy-done((bf16[8,64,256]{2,1,0:T(8,128)(2,1)S(1)}, bf16[8,64,256]{2,1,0:T(8,128)(2,1)}, u32[]{:S(2)}) %copy-start.2) | copy-done | bytes 262168
  3.9 0.0 copy-start.3
  3.9 0.9 %copy-done.3 = bf16[8,64,256]{2,1,0:T(8,128)(2,1)S(1)} copy-done((bf16[8,64,256]{2,1,0:T(8,128)(2,1)S(1)}, bf16[8,64,256]{2,1,0:T(8,128)(2,1)}, u32[]{:S(2)}) %copy-start.3) | copy-done | bytes 262168
  4.9 58.6 %shard_map.73 = f32[64,256]{1,0:T(8,128)S(1)} custom-call(bf16[192,1024]{1,0:T(8,128)(2,1)S(1)} %copy-done.1, bf16[1024,256]{1,0:T(8,128)(2,1)S(1)} %copy-done, bf16[192,256]{1,0:T(8,128)(2,1)S(1)} %copy-done.4, s32[192,16]{1,0:T(8,128)S(1)} %copy.8.mask_hbm, f32[1,256]{1,0:T(1,128)S(1)} %bitcast.1, bf16[8,64,256]{2,1,0:T(8,128)(2,1)S(1)} %copy-done.2, ...), custom_call_target="tpu_custom_call" | custom-call | tf_op jit(solution)/shard_map/pallas_call | solution.py:413
  63.4 0.6 copy.10
Async XLA Ops:
  0.0 0.9 %copy-start.4 = (bf16[192,256]{1,0:T(8,128)(2,1)S(1)}, bf16[192,256]{1,0:T(8,128)(2,1)}, u32[]{:S(2)}) copy-start(bf16[192,256]{1,0:T(8,128)(2,1)} %target_hbm.1) | copy-start | bytes 294916
  0.0 0.9 %copy-start.5 = (f32[256]{0:T(256)S(1)}, f32[256]{0:T(256)}, u32[]{:S(2)}) copy-start(f32[256]{0:T(256)} %param.11) | copy-start | bytes 3076
  0.9 1.0 %copy-start = (bf16[1024,256]{1,0:T(8,128)(2,1)S(1)}, bf16[1024,256]{1,0:T(8,128)(2,1)}, u32[]{:S(2)}) copy-start(bf16[1024,256]{1,0:T(8,128)(2,1)} %coef_hbm.1) | copy-start | bytes 1572868
  2.0 1.0 %copy-start.1 = (bf16[192,1024]{1,0:T(8,128)(2,1)S(1)}, bf16[192,1024]{1,0:T(8,128)(2,1)}, u32[]{:S(2)}) copy-start(bf16[192,1024]{1,0:T(8,128)(2,1)} %dosage_hbm.1) | copy-start | bytes 1179652
  3.0 0.9 %copy-start.2 = (bf16[8,64,256]{2,1,0:T(8,128)(2,1)S(1)}, bf16[8,64,256]{2,1,0:T(8,128)(2,1)}, u32[]{:S(2)}) copy-start(bf16[8,64,256]{2,1,0:T(8,128)(2,1)} %steps_hbm.1) | copy-start | bytes 786436
  3.9 0.9 %copy-start.3 = (bf16[8,64,256]{2,1,0:T(8,128)(2,1)S(1)}, bf16[8,64,256]{2,1,0:T(8,128)(2,1)}, u32[]{:S(2)}) copy-start(bf16[8,64,256]{2,1,0:T(8,128)(2,1)} %changes_hbm.1) | copy-start | bytes 786436

commit v2 on v1

--- a/solution.py
+++ b/solution.py
@@ -15,7 +15,8 @@
 UNITS = 12
 OFFSET = [0] + [(s + 1) // 2 if s % 2 else -(s // 2) for s in range(1, ZN)]
 GROUPS = [(0, 4), (4, 4), (8, 4), (12, 4)]
-EARLY = 9
+SENDS = {"near": (8, 7, 6, 5, 4, 3, 2, 1), "pre": (15,), "post": (), 0: (14, 13), 1: (12, 11, 10, 9), 2: (), 3: ()}
+ORDER = (0, 1, 3, 2)
 
 
 def wait_for(ref, sem):
@@ -74,6 +75,7 @@
     coef,
     target,
     mask,
+    mask_rows,
     hist,
     part,
     tiles,
@@ -114,6 +116,7 @@
     g_recv,
     dots_send,
     dots_recv,
+    beyond,
 ):
     z = lax.axis_index("samp")
     v = lax.axis_index("var")
@@ -139,6 +142,26 @@
         return pltpu.make_async_remote_copy(
             src_ref=src, dst_ref=dst, send_sem=send, recv_sem=recv, device_id=(zz, vv), device_id_type=MESH
         )
+
+    coming, leaving = {}, []
+
+    def take(name):
+        coming.pop(name)()
+
+    def finish():
+        for name in list(coming):
+            take(name)
+        for left in leaving:
+            left()
+
+    barrier = pltpu.get_barrier_semaphore()
+
+    for r in (4, 12, 3, 13, 2, 14, 1, 15):
+        pl.semaphore_signal(barrier, inc=1, device_id=(lax.rem(z + r, ZN), v), device_id_type=MESH)
+
+    @pl.loop(1, VN)
+    def _(r):
+        pl.semaphore_signal(barrier, inc=1, device_id=(z, lax.rem(v + r, VN)), device_id_type=MESH)
 
     loads = [
         pltpu.make_async_copy(dosage_hbm, dosage, local_sem.at[0]),
@@ -150,16 +173,6 @@
     ]
     for load in loads:
         load.start()
-
-    barrier = pltpu.get_barrier_semaphore()
-
-    @pl.loop(1, VN)
-    def _(r):
-        pl.semaphore_signal(barrier, inc=1, device_id=(z, lax.rem(v + r, VN)), device_id_type=MESH)
-
-    @pl.loop(1, ZN)
-    def _(r):
-        pl.semaphore_signal(barrier, inc=1, device_id=(lax.rem(z + r, ZN), v), device_id_type=MESH)
 
     loads[0].wait()
     loads[1].wait()
@@ -172,10 +185,13 @@
         low = dosage[96:192, 128 * j : 128 * j + 128]
         tiles[2 * j] = jnp.concatenate([top[:, :64], low[:, :64]], axis=1)
         tiles[2 * j + 1] = jnp.concatenate([top[:, 64:], low[:, 64:]], axis=1)
-    loads[2].wait()
-    loads[3].wait()
-
-    pl.semaphore_wait(barrier, VN - 1 + ZN - 1)
+    for load in loads[2:]:
+        load.wait()
+    mask_rows[...] = mask[...].astype(jnp.float32).T
+
+    pl.semaphore_wait(barrier, VN - 1 + 8)
+    for r in (4, 12):
+        pl.semaphore_signal(beyond, inc=1, device_id=(lax.rem(z + r, ZN), v), device_id_type=MESH)
 
     @pl.loop(1, VN)
     def _(r):
@@ -186,14 +202,42 @@
         def _():
             remote(part.at[u, lax.rem(dest, 2)], partial_in.at[VN - 1 - r], part_send, part_recv, z, dest).start()
 
+    def part_left():
+        @pl.when(owner)
+        def _():
+            wait_for(part.at[pl.ds(0, UNITS - 1)], part_send)
+            wait_for(part.at[0, 0], part_send)
+
+        @pl.when(jnp.logical_not(owner))
+        def _():
+            wait_for(part, part_send)
+
+    def part_here():
+        @pl.when(owner)
+        def _():
+            wait_for(partial_in, part_recv)
+
+    leaving.append(part_left)
+    coming["part"] = part_here
+
     def send_dosage(s):
         g = s // 4
         remote(tiles.at[at_z(s)], x_all.at[core, s], dose_send, dose_recv.at[g], at_z(s), v).start()
-
-    for s in range(1, EARLY):
+        leaving.append(lambda: wait_for(tiles.at[0], dose_send))
+
+    def dosage_here(g):
+        first, count = GROUPS[g]
+        skip = 1 if g == 0 else 0
+        wait_for(x_all.at[core, pl.ds(first + skip, count - skip)], dose_recv.at[g])
+
+    for s in SENDS["near"]:
         send_dosage(s)
+    for g in range(4):
+        coming["dose%d" % g] = functools.partial(dosage_here, g)
     hist_copy = remote(hist.at[:, :, other_lanes], hist_other, hist_send, hist_recv, z, mate)
     hist_copy.start()
+    leaving.append(hist_copy.wait_send)
+    coming["hist"] = hist_copy.wait_recv
 
     gram_acc[...] = jnp.zeros_like(gram_acc)
     half = PAIRS * (PAIRS + 1) // 2
@@ -219,6 +263,7 @@
         precision=lax.Precision.HIGHEST,
         preferred_element_type=jnp.float32,
     )[0:1]
+    x_all[core, 0] = tiles[z]
 
     @pl.loop(1, VN)
     def _(r):
@@ -226,80 +271,104 @@
             gram_own.at[0], gram_plane.at[VN - 1 - r], gram_send, gram_recv, z, lax.rem(v + r, VN)
         ).start()
 
-    x_all[core, 0] = tiles[z]
-    loads[4].wait()
-    loads[5].wait()
-
-    def spread(groups_from, count, g):
+    leaving.append(lambda: wait_for(gram_plane, gram_send))
+    coming["gram"] = lambda: wait_for(gram_plane, gram_recv)
+    pl.semaphore_wait(beyond, 2)
+    for s in SENDS["pre"]:
+        send_dosage(s)
+
+    def spread(first, count, g):
         @pl.loop(1, VN // 2)
         def _(r):
-            block = r_all.at[pl.ds(groups_from, count), mine]
+            block = r_all.at[pl.ds(first, count), mine]
             remote(block, block, res_send.at[1], res_recv.at[4 + g], z, lax.rem(v + 2 * r, VN)).start()
+
+    def residuals_here(first, count, g):
+        @pl.when(owner)
+        def _():
+            wait_for(r_all.at[pl.ds(first, count), pl.ds(0, UNITS - 1)], res_recv.at[4 + g])
+
+        @pl.when(jnp.logical_not(owner))
+        def _():
+            wait_for(r_all.at[pl.ds(first, count)], res_recv.at[4 + g])
+
+    def line_here(g):
+        first, count = GROUPS[g]
+        skip = 1 if g == 0 else 0
+
+        @pl.when(owner)
+        def _():
+            wait_for(r_all.at[pl.ds(first + skip, count - skip), mine], res_recv.at[g])
+
+    def when_owner(what):
+        @pl.when(owner)
+        def _():
+            what()
+
+    take("part")
 
     @pl.when(owner)
     def _():
         rows = pl.ds(pl.multiple_of(mine * 16, 16), 16)
         lane = lax.broadcasted_iota(jnp.int32, (16, 128), 1)
         word_at = jnp.right_shift(lane, 4) + 8 * core
-        words = mask[rows, :]
+        words = mask_rows[rows, :].astype(jnp.int32)
         word = jnp.zeros((16, 128), jnp.int32)
         for w in range(16):
             word = jnp.where(word_at == w, jnp.broadcast_to(words[:, w : w + 1], (16, 128)), word)
         observed = jnp.bitwise_and(jnp.right_shift(word, jnp.bitwise_and(lane, 15)), 1).astype(jnp.float32)
         wanted = target[rows, lanes].astype(jnp.float32)
-        wait_for(partial_in, part_recv)
         margin = (row_sum(partial_in[...]) + part[mine, core]) * scale
         r_all[0, mine] = (observed * (margin - wanted)).astype(jnp.bfloat16)
         for s in range(1, ZN):
             remote(r_all.at[0, mine], r_all.at[s, mine], res_send.at[0], res_recv.at[s // 4], at_z(s), v).start()
         spread(0, 1, 0)
 
-    for s in range(EARLY, ZN):
-        send_dosage(s)
-
-    wait_for(gram_plane, gram_recv)
+    leaving.append(lambda: when_owner(lambda: wait_for(r_all.at[pl.ds(1, ZN - 1), 0], res_send.at[0])))
+    leaving.append(lambda: when_owner(lambda: wait_for(r_all.at[pl.ds(1, ZN - 1), 0], res_send.at[1])))
+    for g in range(4):
+        coming["line%d" % g] = functools.partial(line_here, g)
+    coming["res0"] = lambda: residuals_here(0, 1, 0)
+
+    take("gram")
     gram_own[1] = row_sum(gram_plane[...]) + gram_own[0]
     for s in range(1, ZN):
         remote(gram_own.at[1], gram_line.at[s - 1], line_send.at[0], line_recv.at[0], at_z(s), v).start()
+    leaving.append(lambda: wait_for(gram_line, line_send.at[0]))
+    coming["gram_line"] = lambda: wait_for(gram_line, line_recv.at[0])
+    for s in SENDS["post"]:
+        send_dosage(s)
 
     def swap(g):
         first, count = GROUPS[g]
-        skip = 1 if g == 0 else 0
-        wait_for(x_all.at[core, pl.ds(first + skip, count - skip)], dose_recv.at[g])
+        take("dose%d" % g)
         block = x_all.at[core, pl.ds(first, count)]
         remote(block, block, swap_send, swap_recv.at[g], z, mate).start()
+        leaving.append(lambda: wait_for(x_all.at[0, pl.ds(first, count)], swap_send))
+        coming["swap%d" % g] = lambda: wait_for(x_all.at[other, pl.ds(first, count)], swap_recv.at[g])
 
     def pass_on(g):
         first, count = GROUPS[g]
         skip = 1 if g == 0 else 0
-
-        @pl.when(owner)
-        def _():
-            wait_for(r_all.at[pl.ds(first + skip, count - skip), mine], res_recv.at[g])
-            spread(first + skip, count - skip, g + 1)
+        take("line%d" % g)
+        when_owner(lambda: spread(first + skip, count - skip, g + 1))
+        for _ in range(count - skip):
+            leaving.append(lambda: when_owner(lambda: wait_for(r_all.at[pl.ds(1, ZN - 1), 0], res_send.at[1])))
+        coming["res%d" % (g + 1)] = lambda: residuals_here(first + skip, count - skip, g + 1)
+        for s in SENDS[g]:
+            send_dosage(s)
 
     def turn(g):
         first, count = GROUPS[g]
-        wait_for(x_all.at[other, pl.ds(first, count)], swap_recv.at[g])
+        take("swap%d" % g)
         for c in range(2):
             x_turned[c, g] = x_all[c, first : first + count].reshape(count * 96, 128).T
-
-    def residuals_here(first, count, g):
-        @pl.when(owner)
-        def _():
-            wait_for(r_all.at[pl.ds(first, count), pl.ds(0, UNITS - 1)], res_recv.at[4 + g])
-
-        @pl.when(jnp.logical_not(owner))
-        def _():
-            wait_for(r_all.at[pl.ds(first, count)], res_recv.at[4 + g])
 
     def multiply(g):
         first, count = GROUPS[g]
         if g == 0:
-            residuals_here(0, 1, 0)
-            residuals_here(1, count - 1, 1)
-        else:
-            residuals_here(first, count, g + 1)
+            take("res0")
+        take("res%d" % (g + 1))
         rows = jnp.concatenate(
             [
                 r_all[first : first + count, 0:6].reshape(count * 96, 128),
@@ -311,32 +380,31 @@
             total = jnp.dot(x_turned[c, g], rows, preferred_element_type=jnp.float32)
             g_acc[c] = total if g == 0 else g_acc[c] + total
 
-    swap(0)
-    swap(1)
-    pass_on(0)
-    pass_on(1)
-    turn(0)
-    pass_on(2)
-    turn(1)
-    pass_on(3)
-    multiply(0)
-    multiply(1)
-    swap(2)
-    swap(3)
-    turn(2)
-    multiply(2)
-    turn(3)
-    multiply(3)
+    for g in range(4):
+        pass_on(g)
+    take("gram_line")
+    scaling, rows = weight_rows(row_sum(gram_line[...]) + gram_own[1])
+    gamma[...] = scaling
+    for i in range(2 * PAIRS):
+        weights[i : i + 1, :] = rows[i]
+    for g in ORDER:
+        swap(g)
+    for g in ORDER:
+        turn(g)
+    for g in range(4):
+        multiply(g)
 
     for c in range(2):
         total = g_acc[c]
         g_half[c] = (total[:64, :128] + total[64:, 128:]) * scale
     g_copy = remote(g_half.at[other], g_own.at[core], g_send, g_recv, z, mate)
     g_copy.start()
+    leaving.append(g_copy.wait_send)
+    coming["g"] = g_copy.wait_recv
     g_own[core] = g_half[core]
 
     near, far = g_half[core], g_half[other]
-    hist_copy.wait_recv()
+    take("hist")
     sub = lax.broadcasted_iota(jnp.int32, (16, 128), 0)
     lane = lax.broadcasted_iota(jnp.int32, (16, 128), 1)
     folds = []
@@ -347,15 +415,12 @@
     dots_own[0] = jnp.sum(jnp.where(sub == lane, sums, 0.0), axis=0, keepdims=True)
     for s in range(1, ZN):
         remote(dots_own.at[0], dots_line.at[s - 1], line_send.at[1], line_recv.at[1], at_z(s), v).start()
-
-    wait_for(gram_line, line_recv.at[0])
-    scaling, rows = weight_rows(row_sum(gram_line[...]) + gram_own[1])
-    gamma[...] = scaling
-    for i in range(2 * PAIRS):
-        weights[i : i + 1, :] = rows[i]
-    g_copy.wait_recv()
-
-    wait_for(dots_line, line_recv.at[1])
+    leaving.append(lambda: wait_for(dots_line, line_send.at[1]))
+    coming["dots_line"] = lambda: wait_for(dots_line, line_recv.at[1])
+
+    take("g")
+
+    take("dots_line")
     dots_mid[0] = row_sum(dots_line[...]) + dots_own[0]
 
     @pl.loop(1, VN)
@@ -364,13 +429,16 @@
             dots_mid.at[0], dots_plane.at[VN - 1 - r], dots_send, dots_recv, z, lax.rem(v + r, VN)
         ).start()
 
+    leaving.append(lambda: wait_for(dots_plane, dots_send))
+    coming["dots"] = lambda: wait_for(dots_plane, dots_recv)
+
     own_rows = pl.ds(pl.multiple_of(z * 64, 64), 64)
     start = coef[own_rows, :].astype(jnp.float32)
     gradient = jnp.concatenate([g_own[0], g_own[1]], axis=1)
     start = start - STEP * (gamma[0:1, 0:1] * gradient)
     limit = STEP * penalty_ref[...]
 
-    wait_for(dots_plane, dots_recv)
+    take("dots")
     dots = row_sum(dots_plane[...]) + dots_mid[0]
     mix = jnp.sum(weights[...] * dots, axis=1, keepdims=True)
     along = mix[0:1] * hist[0].astype(jnp.float32)
@@ -378,28 +446,7 @@
         along = along + mix[i : i + 1] * hist[i].astype(jnp.float32)
     moved = start - STEP * along
     out_ref[...] = moved - jnp.clip(moved, -limit, limit)
-
-    @pl.when(owner)
-    def _():
-        wait_for(part.at[pl.ds(0, UNITS - 1)], part_send)
-        wait_for(part.at[0, 0], part_send)
-        wait_for(r_all.at[pl.ds(1, ZN - 1), 0], res_send.at[0])
-        wait_for(r_all.at[pl.ds(0, ZN - 1), 0], res_send.at[1])
-        for _ in range(ZN - 1):
-            wait_for(r_all.at[pl.ds(1, ZN - 1), 0], res_send.at[1])
-
-    @pl.when(jnp.logical_not(owner))
-    def _():
-        wait_for(part, part_send)
-
-    wait_for(tiles.at[pl.ds(1, ZN - 1)], dose_send)
-    wait_for(x_all.at[0], swap_send)
-    hist_copy.wait_send()
-    g_copy.wait_send()
-    wait_for(gram_plane, gram_send)
-    wait_for(gram_line, line_send.at[0])
-    wait_for(dots_line, line_send.at[1])
-    wait_for(dots_plane, dots_send)
+    finish()
 
 
 def per_device(dosage, coefficients, targets, mask_words, penalty, past_steps, past_changes):
@@ -419,7 +466,8 @@
             vmem((samples, variants), bf16),
             vmem((variants, traits), bf16),
             vmem((samples, traits), bf16),
-            vmem(mask_words.shape, jnp.int32),
+            vmem(mask_words.shape[::-1], jnp.int32),
+            vmem(mask_words.shape, f32),
             vmem((2 * PAIRS, owned, traits), bf16),
             vmem((UNITS, 2, 16, 128), f32),
             vmem((ZN, 96, 128), bf16),
@@ -460,11 +508,12 @@
             dma,
             dma,
             dma,
+            pltpu.SemaphoreType.REGULAR,
         ],
         compiler_params=pltpu.CompilerParams(
-            collective_id=0, has_side_effects=True, vmem_limit_bytes=48 * 1024 * 1024
+            collective_id=0, has_side_effects=True, vmem_limit_bytes=60 * 1024 * 1024
         ),
-    )(dosage, coefficients, targets, mask_words, penalty[None, :], past_steps, past_changes)
+    )(dosage, coefficients, targets, mask_words.T, penalty[None, :], past_steps, past_changes)
 
 
 def solution(mesh):

time: 64.4 us -> 56 us (0.87)
  Pallas kernels: 58.6 us -> 54.3 us
  local copies, waits for them, and re-layouts: 5.48 us -> 1.47 us
    pallas_call x1, Pallas kernels: 58.6 us -> 54.3 us  [per_device(): pl.pallas_call(kernel, out_shape=jax.ShapeDtypeStruct((owned, traits), f3...]
    unnamed x14 -> x1, local copies, waits for them, and re-layouts: 5.48 us -> 1.47 us
where the time goes in v2:
time: 56 us; the launch traced here: 55.8 us
  Pallas kernels  54.3 us (97%)
  local copies, waits for them, and re-layouts  1.47 us (3%)
    pallas_call x1, Pallas kernels, per_device(): pl.pallas_call(kernel, out_shape=jax.ShapeDtypeStruct((owned, traits), f3...  54.3 us
    unnamed x1, local copies, waits for them, and re-layouts  1.47 us

profile of v2, /device:TPU:1, one launch (start us, length us, event | category | flops | bytes accessed | tf_op | source)
XLA Modules:
  0.0 55.8 jit_solution(10642499846921732790)
XLA Ops:
  0.0 54.3 %shard_map.73 = f32[64,256]{1,0:T(8,128)} custom-call(bf16[192,1024]{1,0:T(8,128)(2,1)} %dosage_hbm.1, bf16[1024,256]{1,0:T(8,128)(2,1)} %coef_hbm.1, bf16[192,256]{1,0:T(8,128)(2,1)} %target_hbm.1, s32[16,192]{1,0:T(8,128)} %bitcast.2, f32[1,256]{1,0:T(1,128)} %bitcast.3, bf16[8,64,256]{2,1,0:T(8,128)(2,1)} %steps_hbm.1, bf16[8,64,256]{2,1,0:T(8,128)(2,1)} %changes_hbm.1), custom_call_target="tpu_custom_call" | custom-call | tf_op jit(solution)/shard_map/pallas_call | solution.py:460
  54.3 1.5 %copy.9 = f32[64,256]{1,0:T(8,128)} copy(f32[64,256]{1,0:T(8,128)} %shard_map.73) | data formatting | bytes 131072

commit v3 on v2

--- a/solution.py
+++ b/solution.py
@@ -193,14 +193,15 @@
     for r in (4, 12):
         pl.semaphore_signal(beyond, inc=1, device_id=(lax.rem(z + r, ZN), v), device_id_type=MESH)
 
-    @pl.loop(1, VN)
-    def _(r):
-        dest = lax.rem(v + r, VN)
-        owns, u = unit_of(lax.div(dest, 2))
-
-        @pl.when(owns)
-        def _():
-            remote(part.at[u, lax.rem(dest, 2)], partial_in.at[VN - 1 - r], part_send, part_recv, z, dest).start()
+    for u in range(UNITS):
+        x, y = u // 3, (u % 3 - u // 3) % 4
+        for h in range(2):
+            dest = 2 * (4 * x + y) + h
+
+            @pl.when(v != dest)
+            def _():
+                place = lax.rem(v - dest + VN, VN) - 1
+                remote(part.at[u, h], partial_in.at[place], part_send, part_recv, z, dest).start()
 
     def part_left():
         @pl.when(owner)
@@ -511,7 +512,7 @@
             pltpu.SemaphoreType.REGULAR,
         ],
         compiler_params=pltpu.CompilerParams(
-            collective_id=0, has_side_effects=True, vmem_limit_bytes=60 * 1024 * 1024
+            collective_id=0, has_side_effects=True, vmem_limit_bytes=55130 * 1024
         ),
     )(dosage, coefficients, targets, mask_words.T, penalty[None, :], past_steps, past_changes)
 

time: 56 us -> 55.2 us (0.986)
  Pallas kernels: 54.3 us -> 52.9 us
    pallas_call x1, Pallas kernels: 54.3 us -> 52.9 us  [per_device(): pl.pallas_call(kernel, out_shape=jax.ShapeDtypeStruct((owned, traits), f3...]
    unnamed x1 -> x5, local copies, waits for them, and re-layouts: 1.47 us -> 2.03 us
where the time goes in v3:
time: 55.2 us; the launch traced here: 55 us
  Pallas kernels  52.9 us (96%)
  local copies, waits for them, and re-layouts  2.03 us (4%)
    pallas_call x1, Pallas kernels, per_device(): pl.pallas_call(kernel, out_shape=jax.ShapeDtypeStruct((owned, traits), f3...  52.9 us
    unnamed x5, local copies, waits for them, and re-layouts  2.03 us

profile of v3, /device:TPU:1, one launch (start us, length us, event | category | flops | bytes accessed | tf_op | source)
XLA Modules:
  0.0 55.0 jit_solution(18007116358237371700)
XLA Ops:
  0.0 0.0 copy-start.1
  0.0 0.7 %copy-done.1 = f32[256]{0:T(256)S(1)} copy-done((f32[256]{0:T(256)S(1)}, f32[256]{0:T(256)}, u32[]{:S(2)}) %copy-start.1) | copy-done | bytes 1048
  0.7 0.0 copy-start
  0.7 0.7 %copy-done = s32[192,16]{0,1:T(8,128)S(1)} copy-done((s32[192,16]{0,1:T(8,128)S(1)}, s32[192,16]{0,1:T(8,128)}, u32[]{:S(2)}) %copy-start) | copy-done | bytes 12312
  1.4 52.9 %shard_map.73 = f32[64,256]{1,0:T(8,128)S(1)} custom-call(bf16[192,1024]{1,0:T(8,128)(2,1)} %dosage_hbm.1, bf16[1024,256]{1,0:T(8,128)(2,1)} %coef_hbm.1, bf16[192,256]{1,0:T(8,128)(2,1)} %target_hbm.1, s32[16,192]{1,0:T(8,128)S(1)} %bitcast.2, f32[1,256]{1,0:T(1,128)S(1)} %bitcast.3, bf16[8,64,256]{2,1,0:T(8,128)(2,1)} %steps_hbm.1, ...), custom_call_target="tpu_custom_call" | custom-call | tf_op jit(solution)/shard_map/pallas_call | solution.py:461
  54.3 0.6 %copy.9 = f32[64,256]{1,0:T(8,128)} copy(f32[64,256]{1,0:T(8,128)S(1)} %shard_map.73) | data formatting | bytes 131072
Async XLA Ops:
  0.0 0.7 %copy-start.1 = (f32[256]{0:T(256)S(1)}, f32[256]{0:T(256)}, u32[]{:S(2)}) copy-start(f32[256]{0:T(256)} %param.11) | copy-start | bytes 3076
  0.7 0.7 %copy-start = (s32[192,16]{0,1:T(8,128)S(1)}, s32[192,16]{0,1:T(8,128)}, u32[]{:S(2)}) copy-start(s32[192,16]{0,1:T(8,128)} %param.10) | copy-start | bytes 36868

commit v4 on v3

--- a/solution.py
+++ b/solution.py
@@ -266,14 +266,6 @@
     )[0:1]
     x_all[core, 0] = tiles[z]
 
-    @pl.loop(1, VN)
-    def _(r):
-        remote(
-            gram_own.at[0], gram_plane.at[VN - 1 - r], gram_send, gram_recv, z, lax.rem(v + r, VN)
-        ).start()
-
-    leaving.append(lambda: wait_for(gram_plane, gram_send))
-    coming["gram"] = lambda: wait_for(gram_plane, gram_recv)
     pl.semaphore_wait(beyond, 2)
     for s in SENDS["pre"]:
         send_dosage(s)
@@ -331,14 +323,14 @@
         coming["line%d" % g] = functools.partial(line_here, g)
     coming["res0"] = lambda: residuals_here(0, 1, 0)
 
-    take("gram")
-    gram_own[1] = row_sum(gram_plane[...]) + gram_own[0]
-    for s in range(1, ZN):
-        remote(gram_own.at[1], gram_line.at[s - 1], line_send.at[0], line_recv.at[0], at_z(s), v).start()
-    leaving.append(lambda: wait_for(gram_line, line_send.at[0]))
-    coming["gram_line"] = lambda: wait_for(gram_line, line_recv.at[0])
-    for s in SENDS["post"]:
-        send_dosage(s)
+    @pl.loop(1, VN)
+    def _(r):
+        remote(
+            gram_own.at[0], gram_plane.at[VN - 1 - r], gram_send, gram_recv, z, lax.rem(v + r, VN)
+        ).start()
+
+    leaving.append(lambda: wait_for(gram_plane, gram_send))
+    coming["gram"] = lambda: wait_for(gram_plane, gram_recv)
 
     def swap(g):
         first, count = GROUPS[g]
@@ -383,11 +375,14 @@
 
     for g in range(4):
         pass_on(g)
-    take("gram_line")
-    scaling, rows = weight_rows(row_sum(gram_line[...]) + gram_own[1])
-    gamma[...] = scaling
-    for i in range(2 * PAIRS):
-        weights[i : i + 1, :] = rows[i]
+    take("gram")
+    gram_own[1] = row_sum(gram_plane[...]) + gram_own[0]
+    for s in range(1, ZN):
+        remote(gram_own.at[1], gram_line.at[s - 1], line_send.at[0], line_recv.at[0], at_z(s), v).start()
+    leaving.append(lambda: wait_for(gram_line, line_send.at[0]))
+    coming["gram_line"] = lambda: wait_for(gram_line, line_recv.at[0])
+    for s in SENDS["post"]:
+        send_dosage(s)
     for g in ORDER:
         swap(g)
     for g in ORDER:
@@ -419,6 +414,11 @@
     leaving.append(lambda: wait_for(dots_line, line_send.at[1]))
     coming["dots_line"] = lambda: wait_for(dots_line, line_recv.at[1])
 
+    take("gram_line")
+    scaling, rows = weight_rows(row_sum(gram_line[...]) + gram_own[1])
+    gamma[...] = scaling
+    for i in range(2 * PAIRS):
+        weights[i : i + 1, :] = rows[i]
     take("g")
 
     take("dots_line")

time: 55.2 us -> 55 us (level)
  no operation moved by 1% of the time
where the time goes in v4:
time: 55 us; the launch traced here: 54.8 us
  Pallas kernels  52.8 us (96%)
  local copies, waits for them, and re-layouts  2.03 us (4%)
    pallas_call x1, Pallas kernels, per_device(): pl.pallas_call(kernel, out_shape=jax.ShapeDtypeStruct((owned, traits), f3...  52.8 us
    unnamed x5, local copies, waits for them, and re-layouts  2.03 us

profile of v4, /device:TPU:1, one launch (start us, length us, event | category | flops | bytes accessed | tf_op | source)
XLA Modules:
  0.0 54.8 jit_solution(10586585653074555001)
XLA Ops:
  0.0 0.0 copy-start.1
  0.0 0.7 %copy-done.1 = f32[256]{0:T(256)S(1)} copy-done((f32[256]{0:T(256)S(1)}, f32[256]{0:T(256)}, u32[]{:S(2)}) %copy-start.1) | copy-done | bytes 1048
  0.7 0.0 copy-start
  0.7 0.7 %copy-done = s32[192,16]{0,1:T(8,128)S(1)} copy-done((s32[192,16]{0,1:T(8,128)S(1)}, s32[192,16]{0,1:T(8,128)}, u32[]{:S(2)}) %copy-start) | copy-done | bytes 12312
  1.4 52.8 %shard_map.73 = f32[64,256]{1,0:T(8,128)S(1)} custom-call(bf16[192,1024]{1,0:T(8,128)(2,1)} %dosage_hbm.1, bf16[1024,256]{1,0:T(8,128)(2,1)} %coef_hbm.1, bf16[192,256]{1,0:T(8,128)(2,1)} %target_hbm.1, s32[16,192]{1,0:T(8,128)S(1)} %bitcast.2, f32[1,256]{1,0:T(1,128)S(1)} %bitcast.3, bf16[8,64,256]{2,1,0:T(8,128)(2,1)} %steps_hbm.1, ...), custom_call_target="tpu_custom_call" | custom-call | tf_op jit(solution)/shard_map/pallas_call | solution.py:461
  54.2 0.6 %copy.9 = f32[64,256]{1,0:T(8,128)} copy(f32[64,256]{1,0:T(8,128)S(1)} %shard_map.73) | data formatting | bytes 131072
Async XLA Ops:
  0.0 0.7 %copy-start.1 = (f32[256]{0:T(256)S(1)}, f32[256]{0:T(256)}, u32[]{:S(2)}) copy-start(f32[256]{0:T(256)} %param.11) | copy-start | bytes 3076
  0.7 0.7 %copy-start = (s32[192,16]{0,1:T(8,128)S(1)}, s32[192,16]{0,1:T(8,128)}, u32[]{:S(2)}) copy-start(s32[192,16]{0,1:T(8,128)} %param.10) | copy-start | bytes 36868
